TPU v7x, 128 devices: a whole 4x4x4 slice. The times are simulated.
128 devices in a mesh: rep: 4 (over y_lo, core), gx: 8 (over z, y_hi), gy: 4 (over x).
Axes of the slice: x: 4, y: 4 (y_hi: 2, y_lo: 2; y = y_hi * 2 + y_lo), z: 4, core: 2. Of those that a mesh axis runs over, the one named last changes fastest.
Arguments:
- node_feat: bfloat16 [32768, 256], P(('rep', 'gx', 'gy')), may hold values from -6 to 6
- edge_feat: bfloat16 [1048576, 256], P(('rep', 'gx', 'gy')), may hold values from -6 to 6
- edge_src: int32 [1048576], P(('rep', 'gx', 'gy')), may hold values from 0 to 1023
- edge_dst: int32 [1048576], P(('rep', 'gx', 'gy')), may hold values from 0 to 255
- edge_count: int32 [128], P(('rep', 'gx', 'gy')), may hold values from 2048 to 8192, as said below
- send_idx: int32 [4, 8, 4, 2, 2, 64], P('rep', 'gx', 'gy'), may hold values from 0 to 255
- w_qkv: bfloat16 [2, 256, 768], replicated, may hold values from -0.375 to 0.375
- w_edge: bfloat16 [2, 256, 256], replicated, may hold values from -0.375 to 0.375
- gains: float32 [2, 256], replicated, may hold values from 0.1 to 1.9
- head_in: bfloat16 [256, 256], replicated, may hold values from -0.375 to 0.375
- head_out: bfloat16 [256, 169], replicated, may hold values from -0.375 to 0.375
- targets: bfloat16 [169, 1048576], P(None, ('rep', 'gx', 'gy')), may hold values from -15 to 15
Outputs:
- node_out: bfloat16 [32768, 256], P(('rep', 'gx', 'gy'))
- grad_head_in: float32 [256, 256], replicated
- grad_head_out: float32 [256, 169], replicated
Inputs may be any that keep to these rules, and one draw needn't show every extreme that they name: `edge_count`: edge slots of a tile at positions from its count on are padding; some tile holds 8192 live edges.
All inputs are finite; a program needn't handle non-finite values.
Results may differ from a plain program's by a relative error of at most 0.0025.
The roundings to bfloat16 on the way count: a program that leaves them out, or rounds other values in their place, can miss the bound.
Values may be sent and summed in bfloat16 or wider, within the bound.
No kernel may reach another device: no remote copies, remote signals or barrier semaphores. Data moves between devices by JAX's collectives and lax.ppermute only.
A program may use at most 128 MiB of HBM per device.

v0:
```python
import math
import jax
import jax.numpy as jnp
from jax import lax
from jax.sharding import PartitionSpec as P

OUTER_CELLS = (
    (0, 0),
    (0, 1),
    (0, 2),
    (0, 3),
    (1, 0),
    (1, 3),
    (2, 0),
    (2, 3),
    (3, 0),
    (3, 1),
    (3, 2),
    (3, 3),
)


def with_halo(x, sides, width):
    for axis, dim in sides:
        count, length = (lax.axis_size(axis), x.shape[dim])
        up = [(i, (i + 1) % count) for i in range(count)]
        down = [(j, i) for i, j in up]
        last = lax.slice_in_dim(x, length - width, length, axis=dim)
        initial = lax.slice_in_dim(x, 0, width, axis=dim)
        before = lax.ppermute(last, axis, up)
        after = lax.ppermute(initial, axis, down)
        x = jnp.concatenate([before, x, after], axis=dim)
    return x


def layer_norm(values):
    centre = values - jnp.mean(values, axis=-1, keepdims=True)
    spread = jnp.mean(centre * centre, axis=-1, keepdims=True)
    return centre * lax.rsqrt(spread + 1e-05)


def outer_rows(padded):
    return jnp.concatenate([padded[cell_i, cell_j] for cell_i, cell_j in OUTER_CELLS], axis=0)


def edge_pass(table, query_part, edges, edge_src, edge_dst, live_column, weight_edge):
    edge_slots, feature_width = edges.shape
    atom_count = query_part.shape[0]
    table_rows = table.shape[0]
    block_rows = math.gcd(edge_slots, 2048)
    block_count = edge_slots // block_rows
    table_iota = jnp.arange(table_rows, dtype=jnp.int32)
    atom_iota = jnp.arange(atom_count, dtype=jnp.int32)

    def one_block(carry, items):
        edge_rows, source_rows, target_rows, live_rows = items
        source_hot = (source_rows[:, None] == table_iota[None, :]).astype(jnp.bfloat16)
        target_hot = (target_rows[:, None] == atom_iota[None, :]).astype(jnp.bfloat16)
        gathered = jnp.dot(source_hot, table, preferred_element_type=jnp.float32)
        queries = jnp.dot(target_hot, query_part, preferred_element_type=jnp.float32)
        pre_act = queries + gathered[:, :feature_width]
        pre_act = pre_act + jnp.dot(edge_rows, weight_edge, preferred_element_type=jnp.float32)
        new_rows = (edge_rows.astype(jnp.float32) + live_rows * jax.nn.silu(pre_act)).astype(
            jnp.bfloat16
        )
        weighted = live_rows * jax.nn.sigmoid(pre_act) * gathered[:, feature_width:]
        added = lax.dot_general(
            target_hot.astype(jnp.float32),
            weighted,
            (((0,), (0,)), ((), ())),
            precision=lax.Precision.HIGHEST,
            preferred_element_type=jnp.float32,
        )
        return (carry + added, new_rows)

    start = jnp.zeros((atom_count, feature_width), jnp.float32)
    items = (
        edges.reshape(block_count, block_rows, feature_width),
        edge_src.reshape(block_count, block_rows),
        edge_dst.reshape(block_count, block_rows),
        live_column.reshape(block_count, block_rows, 1),
    )
    summed, new_blocks = lax.scan(one_block, start, items)
    return (summed, new_blocks.reshape(edge_slots, feature_width))


def body(
    node_feat,
    edge_feat,
    edge_src,
    edge_dst,
    edge_count,
    send_idx,
    w_qkv,
    w_edge,
    gains,
    head_in,
    head_out,
    targets,
):
    feature_width = node_feat.shape[1]
    edge_slots = edge_feat.shape[0]
    cell_rows = send_idx.shape[-1]
    corner_index = send_idx.reshape(2, 2, cell_rows)
    positions = jnp.arange(edge_slots, dtype=jnp.int32)
    live_column = (positions < edge_count[0]).astype(jnp.float32)[:, None]
    nodes = node_feat
    edges = edge_feat
    for layer_index in range(w_qkv.shape[0]):
        weight_qkv = w_qkv[layer_index]
        projected = jnp.dot(nodes, weight_qkv, preferred_element_type=jnp.float32).astype(
            jnp.bfloat16
        )
        local_kv = projected[:, feature_width:]
        padded = with_halo(nodes[corner_index], (("gx", 0), ("gy", 1)), 1)
        ghost_kv = jnp.dot(
            outer_rows(padded), weight_qkv[:, feature_width:], preferred_element_type=jnp.float32
        ).astype(jnp.bfloat16)
        table = jnp.concatenate([local_kv, ghost_kv], axis=0)
        summed, edges = edge_pass(
            table,
            projected[:, :feature_width],
            edges,
            edge_src,
            edge_dst,
            live_column,
            w_edge[layer_index],
        )
        nodes = (nodes.astype(jnp.float32) + gains[layer_index] * layer_norm(summed)).astype(
            jnp.bfloat16
        )
    scale = 0.125 / (edge_slots * lax.axis_size(("rep", "gx", "gy"))) ** 0.5
    act_in = jnp.dot(edges, head_in, preferred_element_type=jnp.float32)
    hidden_head = jax.nn.silu(act_in).astype(jnp.bfloat16)
    pred = lax.dot_general(
        head_out, hidden_head, (((0,), (1,)), ((), ())), preferred_element_type=jnp.float32
    )
    live_row = live_column[:, 0][None, :]
    dpred = (live_row * (pred - targets.astype(jnp.float32)) * scale).astype(jnp.bfloat16)
    dhidden = lax.dot_general(
        dpred, head_out, (((0,), (1,)), ((), ())), preferred_element_type=jnp.float32
    )
    sigmoid_in = jax.nn.sigmoid(act_in)
    dact = (dhidden * sigmoid_in * (1.0 + act_in * (1.0 - sigmoid_in))).astype(jnp.bfloat16)
    grad_in = lax.dot_general(
        edges, dact, (((0,), (0,)), ((), ())), preferred_element_type=jnp.float32
    )
    grad_out = lax.dot_general(
        hidden_head, dpred, (((0,), (1,)), ((), ())), preferred_element_type=jnp.float32
    )
    grad_in, grad_out = lax.psum((grad_in, grad_out), ("rep", "gx", "gy"))
    return (nodes, grad_in, grad_out)


def solution(mesh):
    return jax.shard_map(
        body,
        mesh=mesh,
        in_specs=(
            P(("rep", "gx", "gy"), None),
            P(("rep", "gx", "gy"), None),
            P(("rep", "gx", "gy")),
            P(("rep", "gx", "gy")),
            P(("rep", "gx", "gy")),
            P("rep", "gx", "gy", None, None, None),
            P(),
            P(),
            P(),
            P(),
            P(),
            P(None, ("rep", "gx", "gy")),
        ),
        out_specs=(P(("rep", "gx", "gy"), None), P(), P()),
        check_vma=False,
    )
```

profile of v0, /device:TPU:1, one launch (start us, length us, event | category | flops | bytes accessed | tf_op | source)
XLA Modules:
  0.0 348.6 jit_solution(3398888422495279461)
XLA Ops:
  8.2 1.9 gather_fusion
  10.1 3.8 %collective-permute-start = (bf16[1,2,64,256]{3,2,1,0:T(8,128)(2,1)S(1)}, bf16[1,2,64,256]{3,2,1,0:T(8,128)(2,1)S(1)}, u32[]{:S(2)}, u32[]{:S(2)}) collective-permute-start(bf16[1,2,64,256]{3,2,1,0:T(8,128)(2,1)S(1)} %bitcast.229), channel_id=1, source_target_pairs={{0,4},{4,8},{8,12},{12,16},{16,20},{20,24},{24,28},{28,0},{1,5},{5... | collective-permute-start | bytes 196616 | tf_op jit(solution)/shard_map/ppermute | solution.py:30
  13.9 3.6 %collective-permute-start.1 = (bf16[1,2,64,256]{3,2,1,0:T(8,128)(2,1)S(1)}, bf16[1,2,64,256]{3,2,1,0:T(8,128)(2,1)S(1)}, u32[]{:S(2)}, u32[]{:S(2)}) collective-permute-start(bf16[1,2,64,256]{3,2,1,0:T(8,128)(2,1)S(1)} %bitcast.228), channel_id=1, source_target_pairs={{4,0},{8,4},{12,8},{16,12},{20,16},{24,20},{28,24},{0,28},{5,1},{9... | collective-permute-start | bytes 196616 | tf_op jit(solution)/shard_map/ppermute | solution.py:31
  17.4 1.2 slice_bitcast_fusion
  22.6 1.3 collective-permute-start.2
  24.5 1.5 collective-permute-start.3
  25.9 1.8 collective-permute-done.2
  31.2 1.0 pad_maximum_fusion
  32.3 2.2 broadcast.102.clone
  34.5 61.8 %while.26 = (s32[]{:T(128)}, f32[256,256]{1,0:T(8,128)S(1)}, bf16[4,2048,256]{2,1,0:T(8,128)(2,1)}, s32[4,2048]{1,0:T(4,128)S(1)}, f32[4,2048,1]{1,2,0:T(1,128)S...) while((s32[]{:T(128)}, f32[256,256]{1,0:T(8,128)S(1)}, ...), condition=%wide.region_1.2_spmd.clone, body=%wide.region_0.1_spmd.clone.sunk | while | flops 4306108416 | bytes 55403708 | solution.py:83
  34.6 3.6 %fusion.83 = f32[2048,512]{1,0:T(8,128)S(1)} fusion(bf16[1024,512]{1,0:T(8,128)(2,1)} %get-tuple-element.442, s32[2048]{0:T(1024)S(1)} %bitcast.226), kind=kOutput, calls=%fused_computation.7.clone.1 | convolution fusion | flops 2149580800 | bytes 5251072 | tf_op jit(solution)/shard_map/while/body/eval_jaxpr/dot_general | solution.py:59
  38.2 1.6 convolution_add_fusion.6
  39.9 2.0 copy-done.16
  41.9 2.6 bitcast_dynamic-update-slice_fusion.4
  44.6 5.5 %fusion.84 = f32[256,256]{1,0:T(8,128)S(1)} fusion(f32[2048,512]{1,0:T(8,128)} %copy-done.1, f32[2048,256]{1,0:T(8,128)} %get-tuple-element.395, f32[2048]{0:T(1024)S(1)} %bitcast.223, s32[2048]{0:T(1024)S(1)} %bitcast.219, f32[256,256]{1,0:T(8,128)S(1)} %get-tuple-element.424, pred[]{:T(512)S(6)} %compare.6), kind=kOutput, calls=%fused_computation.17.clone.1 | convolution fusion | flops 1613889536 | bytes 4734977 | tf_op jit(solution)/shard_map/while/body/eval_jaxpr/dot_general | solution.py:67
  50.1 3.6 %fusion.83 = f32[2048,512]{1,0:T(8,128)S(1)} fusion(bf16[1024,512]{1,0:T(8,128)(2,1)} %get-tuple-element.442, s32[2048]{0:T(1024)S(1)} %bitcast.226), kind=kOutput, calls=%fused_computation.7.clone.1 | convolution fusion | flops 2149580800 | bytes 5251072 | tf_op jit(solution)/shard_map/while/body/eval_jaxpr/dot_general | solution.py:59
  53.7 1.6 convolution_add_fusion.6
  55.4 2.0 copy-done.16
  57.4 2.5 bitcast_dynamic-update-slice_fusion.4
  60.0 5.5 %fusion.84 = f32[256,256]{1,0:T(8,128)S(1)} fusion(f32[2048,512]{1,0:T(8,128)} %copy-done.1, f32[2048,256]{1,0:T(8,128)} %get-tuple-element.395, f32[2048]{0:T(1024)S(1)} %bitcast.223, s32[2048]{0:T(1024)S(1)} %bitcast.219, f32[256,256]{1,0:T(8,128)S(1)} %get-tuple-element.424, pred[]{:T(512)S(6)} %compare.6), kind=kOutput, calls=%fused_computation.17.clone.1 | convolution fusion | flops 1613889536 | bytes 4734977 | tf_op jit(solution)/shard_map/while/body/eval_jaxpr/dot_general | solution.py:67
  65.5 3.6 %fusion.83 = f32[2048,512]{1,0:T(8,128)S(1)} fusion(bf16[1024,512]{1,0:T(8,128)(2,1)} %get-tuple-element.442, s32[2048]{0:T(1024)S(1)} %bitcast.226), kind=kOutput, calls=%fused_computation.7.clone.1 | convolution fusion | flops 2149580800 | bytes 5251072 | tf_op jit(solution)/shard_map/while/body/eval_jaxpr/dot_general | solution.py:59
  69.1 1.6 convolution_add_fusion.6
  70.8 2.0 copy-done.16
  72.8 2.6 bitcast_dynamic-update-slice_fusion.4
  75.4 5.5 %fusion.84 = f32[256,256]{1,0:T(8,128)S(1)} fusion(f32[2048,512]{1,0:T(8,128)} %copy-done.1, f32[2048,256]{1,0:T(8,128)} %get-tuple-element.395, f32[2048]{0:T(1024)S(1)} %bitcast.223, s32[2048]{0:T(1024)S(1)} %bitcast.219, f32[256,256]{1,0:T(8,128)S(1)} %get-tuple-element.424, pred[]{:T(512)S(6)} %compare.6), kind=kOutput, calls=%fused_computation.17.clone.1 | convolution fusion | flops 1613889536 | bytes 4734977 | tf_op jit(solution)/shard_map/while/body/eval_jaxpr/dot_general | solution.py:67
  80.9 3.6 %fusion.83 = f32[2048,512]{1,0:T(8,128)S(1)} fusion(bf16[1024,512]{1,0:T(8,128)(2,1)} %get-tuple-element.442, s32[2048]{0:T(1024)S(1)} %bitcast.226), kind=kOutput, calls=%fused_computation.7.clone.1 | convolution fusion | flops 2149580800 | bytes 5251072 | tf_op jit(solution)/shard_map/while/body/eval_jaxpr/dot_general | solution.py:59
  84.6 1.6 convolution_add_fusion.6
  86.2 2.0 copy-done.16
  88.3 2.6 bitcast_dynamic-update-slice_fusion.4
  90.9 5.5 %fusion.84 = f32[256,256]{1,0:T(8,128)S(1)} fusion(f32[2048,512]{1,0:T(8,128)} %copy-done.1, f32[2048,256]{1,0:T(8,128)} %get-tuple-element.395, f32[2048]{0:T(1024)S(1)} %bitcast.223, s32[2048]{0:T(1024)S(1)} %bitcast.219, f32[256,256]{1,0:T(8,128)S(1)} %get-tuple-element.424, pred[]{:T(512)S(6)} %compare.6), kind=kOutput, calls=%fused_computation.17.clone.1 | convolution fusion | flops 1613889536 | bytes 4734977 | tf_op jit(solution)/shard_map/while/body/eval_jaxpr/dot_general | solution.py:67
  96.8 1.2 gather_fusion.1
  98.3 4.8 %collective-permute-start.5 = (bf16[1,2,64,256]{3,2,1,0:T(8,128)(2,1)S(1)}, bf16[1,2,64,256]{3,2,1,0:T(8,128)(2,1)S(1)}, u32[]{:S(2)}, u32[]{:S(2)}) collective-permute-start(bf16[1,2,64,256]{3,2,1,0:T(8,128)(2,1)S(1)} %bitcast.230), channel_id=1, source_target_pairs={{4,0},{8,4},{12,8},{16,12},{20,16},{24,20},{28,24},{0,28},{5,1},{9... | collective-permute-start | bytes 196616 | tf_op jit(solution)/shard_map/ppermute | solution.py:31
  103.2 1.6 collective-permute-done.4
  105.5 2.7 collective-permute-start.7
  108.2 1.8 collective-permute-done.6
  110.7 2.3 broadcast.102
  113.0 56.8 %while.27 = (s32[]{:T(128)}, f32[256,256]{1,0:T(8,128)S(1)}, bf16[4,2048,256]{2,1,0:T(8,128)(2,1)}, s32[4,2048]{1,0:T(4,128)S(1)}, f32[4,2048,1]{1,2,0:T(1,128)S...) while((s32[]{:T(128)}, f32[256,256]{1,0:T(8,128)S(1)}, ...), condition=%wide.region_5.6_spmd.clone, body=%wide.region_4.5_spmd.clone.sunk | while | flops 4306108416 | bytes 55403708 | solution.py:83
  113.0 2.4 fusion.88
  115.4 1.6 convolution_add_fusion.7
  117.0 2.0 copy-done.5
  119.1 2.6 bitcast_dynamic-update-slice_fusion.5
  121.7 5.5 %fusion.89 = f32[256,256]{1,0:T(8,128)S(1)} fusion(f32[2048,512]{1,0:T(8,128)} %copy-done.2, f32[2048,256]{1,0:T(8,128)} %get-tuple-element.409, f32[2048]{0:T(1024)S(1)} %bitcast.225, s32[2048]{0:T(1024)S(1)} %bitcast.221, f32[256,256]{1,0:T(8,128)S(1)} %get-tuple-element.460, pred[]{:T(512)S(6)} %compare.7), kind=kOutput, calls=%fused_computation.41.clone.1 | convolution fusion | flops 1613889536 | bytes 4734977 | tf_op jit(solution)/shard_map/while/body/eval_jaxpr/dot_general | solution.py:67
  127.2 2.4 fusion.88
  129.6 1.6 convolution_add_fusion.7
  131.3 2.0 copy-done.5
  133.3 2.5 bitcast_dynamic-update-slice_fusion.5
  135.9 5.5 %fusion.89 = f32[256,256]{1,0:T(8,128)S(1)} fusion(f32[2048,512]{1,0:T(8,128)} %copy-done.2, f32[2048,256]{1,0:T(8,128)} %get-tuple-element.409, f32[2048]{0:T(1024)S(1)} %bitcast.225, s32[2048]{0:T(1024)S(1)} %bitcast.221, f32[256,256]{1,0:T(8,128)S(1)} %get-tuple-element.460, pred[]{:T(512)S(6)} %compare.7), kind=kOutput, calls=%fused_computation.41.clone.1 | convolution fusion | flops 1613889536 | bytes 4734977 | tf_op jit(solution)/shard_map/while/body/eval_jaxpr/dot_general | solution.py:67
  141.4 2.4 fusion.88
  143.8 1.6 convolution_add_fusion.7
  145.4 2.0 copy-done.5
  147.5 2.6 bitcast_dynamic-update-slice_fusion.5
  150.1 5.5 %fusion.89 = f32[256,256]{1,0:T(8,128)S(1)} fusion(f32[2048,512]{1,0:T(8,128)} %copy-done.2, f32[2048,256]{1,0:T(8,128)} %get-tuple-element.409, f32[2048]{0:T(1024)S(1)} %bitcast.225, s32[2048]{0:T(1024)S(1)} %bitcast.221, f32[256,256]{1,0:T(8,128)S(1)} %get-tuple-element.460, pred[]{:T(512)S(6)} %compare.7), kind=kOutput, calls=%fused_computation.41.clone.1 | convolution fusion | flops 1613889536 | bytes 4734977 | tf_op jit(solution)/shard_map/while/body/eval_jaxpr/dot_general | solution.py:67
  155.6 2.4 fusion.88
  158.0 1.6 convolution_add_fusion.7
  159.7 2.0 copy-done.5
  161.7 2.6 bitcast_dynamic-update-slice_fusion.5
  164.3 5.5 %fusion.89 = f32[256,256]{1,0:T(8,128)S(1)} fusion(f32[2048,512]{1,0:T(8,128)} %copy-done.2, f32[2048,256]{1,0:T(8,128)} %get-tuple-element.409, f32[2048]{0:T(1024)S(1)} %bitcast.225, s32[2048]{0:T(1024)S(1)} %bitcast.221, f32[256,256]{1,0:T(8,128)S(1)} %get-tuple-element.460, pred[]{:T(512)S(6)} %compare.7), kind=kOutput, calls=%fused_computation.41.clone.1 | convolution fusion | flops 1613889536 | bytes 4734977 | tf_op jit(solution)/shard_map/while/body/eval_jaxpr/dot_general | solution.py:67
  169.8 6.9 %multiply_convert_fusion = (bf16[8192,256]{1,0:T(8,128)(2,1)S(1)}, f32[8192,256]{1,0:T(8,128)}) fusion(bf16[8192,256]{1,0:T(8,128)(2,1)} %bitcast.214, bf16[256,256]{1,0:T(8,128)(2,1)S(1)} %copy-done), kind=kOutput, calls=%fused_computation.62 | convolution fusion | flops 1084227584 | bytes 16908288 | tf_op jit(solution)/shard_map/dot_general | solution.py:133
  176.7 1.6 fusion.39
  178.3 1.6 fusion.50
  179.9 9.2 %fusion.40 = f32[256,256]{1,0:T(8,128)} fusion(bf16[8192,256]{1,0:T(8,128)(2,1)} %bitcast.215, bf16[169,8192]{1,0:T(8,128)(2,1)S(1)} %fusion.39, bf16[256,169]{0,1:T(8,128)(2,1)S(1)} %copy-done.18, f32[8192,256]{1,0:T(8,128)} %get-tuple-element.272), kind=kOutput, calls=%fused_computation.64 | convolution fusion | flops 1801453568 | bytes 15700480 | tf_op jit(solution)/shard_map/dot_general | solution.py:145
  190.3 148.2 %all-reduce.3.cloned.1.call-done = (f32[256,256]{1,0:T(8,128)}, f32[256,169]{0,1:T(8,128)}) async-done(((f32[256,256]{1,0:T(8,128)}, f32[256,169]{0,1:T(8,128)}), (f32[256,256]{1,0:T(8,128)}, f32[256,169]{0,1:T(8,128)})) %all-reduce.3.cloned.1.call-update) | async-done | bytes 435216 | tf_op jit(solution)/shard_map/psum | solution.py:151
  338.5 1.7 copy.60
  340.2 1.6 copy.61
  (140 shorter events, 11.7 us)
Async XLA Ops:
  7.2 162.6 %copy-start = (bf16[256,256]{1,0:T(8,128)(2,1)S(1)}, bf16[256,256]{1,0:T(8,128)(2,1)}, u32[]{:S(2)}) copy-start(bf16[256,256]{1,0:T(8,128)(2,1)} %param.25) | copy-start | bytes 393220
  7.2 11.4 %copy-start.3 = (bf16[256,256]{1,0:T(8,128)(2,1)S(1)}, bf16[256,256]{1,0:T(8,128)(2,1)}, u32[]{:S(2)}) copy-start(bf16[256,256]{1,0:T(8,128)(2,1)} %param.16) | copy-start | bytes 393220
  7.2 11.4 %copy-start.6 = (bf16[2,256,768]{2,1,0:T(8,128)(2,1)S(1)}, bf16[2,256,768]{2,1,0:T(8,128)(2,1)}, u32[]{:S(2)}) copy-start(bf16[2,256,768]{2,1,0:T(8,128)(2,1)} %param.22) | copy-start | bytes 2359300
  7.2 12.4 %copy-start.7 = (bf16[2,256,256]{2,1,0:T(8,128)(2,1)S(1)}, bf16[2,256,256]{2,1,0:T(8,128)(2,1)}, u32[]{:S(2)}) copy-start(bf16[2,256,256]{2,1,0:T(8,128)(2,1)} %param.23) | copy-start | bytes 786436
  7.2 13.2 %copy-start.12 = (s32[8192]{0:T(1024)S(1)}, s32[8192]{0:T(1024)}, u32[]{:S(2)}) copy-start(s32[8192]{0:T(1024)} %param.19) | copy-start | bytes 98308
  7.2 13.2 %copy-start.13 = (s32[8192]{0:T(1024)S(1)}, s32[8192]{0:T(1024)}, u32[]{:S(2)}) copy-start(s32[8192]{0:T(1024)} %param.18) | copy-start | bytes 98308
  7.2 331.3 %all-reduce.3.cloned.1.call-start = ((), (), s32[]{:S(2)}) async-start(), calls=%async_computation | async-start | bytes 884736 | tf_op jit(solution)/shard_map/psum | solution.py:151
  10.0 13.9 %copy-start.15 = (f32[2,256]{1,0:T(2,128)S(1)}, f32[2,256]{1,0:T(2,128)}, u32[]{:S(2)}) copy-start(f32[2,256]{1,0:T(2,128)} %param.24) | copy-start | bytes 6148
  10.1 10.4 %collective-permute-start = (bf16[1,2,64,256]{3,2,1,0:T(8,128)(2,1)S(1)}, bf16[1,2,64,256]{3,2,1,0:T(8,128)(2,1)S(1)}, u32[]{:S(2)}, u32[]{:S(2)}) collective-permute-start(bf16[1,2,64,256]{3,2,1,0:T(8,128)(2,1)S(1)} %bitcast.229), channel_id=1, source_target_pairs={{0,4},{4,8},{8,12},{12,16},{16,20},{20,24},{24,28},{28,0},{1,5},{5... | collective-permute-start | bytes 196616 | tf_op jit(solution)/shard_map/ppermute | solution.py:30
  13.9 6.6 %collective-permute-start.1 = (bf16[1,2,64,256]{3,2,1,0:T(8,128)(2,1)S(1)}, bf16[1,2,64,256]{3,2,1,0:T(8,128)(2,1)S(1)}, u32[]{:S(2)}, u32[]{:S(2)}) collective-permute-start(bf16[1,2,64,256]{3,2,1,0:T(8,128)(2,1)S(1)} %bitcast.228), channel_id=1, source_target_pairs={{4,0},{8,4},{12,8},{16,12},{20,16},{24,20},{28,24},{0,28},{5,1},{9... | collective-permute-start | bytes 196616 | tf_op jit(solution)/shard_map/ppermute | solution.py:31
  18.9 13.4 %copy-start.4 = (bf16[256,768]{1,0:T(8,128)(2,1)}, bf16[256,768]{1,0:T(8,128)(2,1)S(1)}, u32[]{:S(2)}) copy-start(bf16[256,768]{1,0:T(8,128)(2,1)S(1)} %convolution_convert_fusion.3) | copy-start | bytes 1179652
  20.5 0.6 copy-start.9
  21.1 0.6 copy-start.8
  22.6 5.1 %collective-permute-start.2 = (bf16[4,1,64,256]{3,2,1,0:T(8,128)(2,1)S(1)}, bf16[4,1,64,256]{3,2,1,0:T(8,128)(2,1)S(1)}, u32[]{:S(2)}, u32[]{:S(2)}) collective-permute-start(bf16[4,1,64,256]{3,2,1,0:T(8,128)(2,1)S(1)} %get-tuple-element.264), channel_id=1, source_target_pairs={{0,1},{1,2},{2,3},{3,0},{4,5},{5,6},{6,7},{7,4},{8,9},{9,10},{10,1... | collective-permute-start | bytes 393224 | tf_op jit(solution)/shard_map/ppermute | solution.py:30
  24.5 4.8 %collective-permute-start.3 = (bf16[4,1,64,256]{3,2,1,0:T(8,128)(2,1)S(1)}, bf16[4,1,64,256]{3,2,1,0:T(8,128)(2,1)S(1)}, u32[]{:S(2)}, u32[]{:S(2)}) collective-permute-start(bf16[4,1,64,256]{3,2,1,0:T(8,128)(2,1)S(1)} %get-tuple-element.263), channel_id=1, source_target_pairs={{1,0},{2,1},{3,2},{0,3},{5,4},{6,5},{7,6},{4,7},{9,8},{10,9},{11,1... | collective-permute-start | bytes 393224 | tf_op jit(solution)/shard_map/ppermute | solution.py:31
  31.2 3.3 copy-start.11
  32.3 2.2 slice-start
  38.2 6.4 %copy-start.1 = (f32[2048,512]{1,0:T(8,128)}, f32[2048,512]{1,0:T(8,128)S(1)}, u32[]{:S(2)}) copy-start(f32[2048,512]{1,0:T(8,128)S(1)} %fusion.83) | copy-start | bytes 12582916 | tf_op jit(solution)/shard_map/while
  38.2 3.7 %copy-start.16 = (bf16[4,2048,256]{2,1,0:T(8,128)(2,1)S(1)}, bf16[4,2048,256]{2,1,0:T(8,128)(2,1)}, u32[]{:S(2)}) copy-start(bf16[4,2048,256]{2,1,0:T(8,128)(2,1)} %get-tuple-element.443) | copy-start | bytes 12582916 | tf_op jit(solution)/shard_map/while
  53.7 6.3 %copy-start.1 = (f32[2048,512]{1,0:T(8,128)}, f32[2048,512]{1,0:T(8,128)S(1)}, u32[]{:S(2)}) copy-start(f32[2048,512]{1,0:T(8,128)S(1)} %fusion.83) | copy-start | bytes 12582916 | tf_op jit(solution)/shard_map/while
  53.7 3.7 %copy-start.16 = (bf16[4,2048,256]{2,1,0:T(8,128)(2,1)S(1)}, bf16[4,2048,256]{2,1,0:T(8,128)(2,1)}, u32[]{:S(2)}) copy-start(bf16[4,2048,256]{2,1,0:T(8,128)(2,1)} %get-tuple-element.443) | copy-start | bytes 12582916 | tf_op jit(solution)/shard_map/while
  69.1 6.3 %copy-start.1 = (f32[2048,512]{1,0:T(8,128)}, f32[2048,512]{1,0:T(8,128)S(1)}, u32[]{:S(2)}) copy-start(f32[2048,512]{1,0:T(8,128)S(1)} %fusion.83) | copy-start | bytes 12582916 | tf_op jit(solution)/shard_map/while
  69.1 3.7 %copy-start.16 = (bf16[4,2048,256]{2,1,0:T(8,128)(2,1)S(1)}, bf16[4,2048,256]{2,1,0:T(8,128)(2,1)}, u32[]{:S(2)}) copy-start(bf16[4,2048,256]{2,1,0:T(8,128)(2,1)} %get-tuple-element.443) | copy-start | bytes 12582916 | tf_op jit(solution)/shard_map/while
  84.5 6.3 %copy-start.1 = (f32[2048,512]{1,0:T(8,128)}, f32[2048,512]{1,0:T(8,128)S(1)}, u32[]{:S(2)}) copy-start(f32[2048,512]{1,0:T(8,128)S(1)} %fusion.83) | copy-start | bytes 12582916 | tf_op jit(solution)/shard_map/while
  84.5 3.7 %copy-start.16 = (bf16[4,2048,256]{2,1,0:T(8,128)(2,1)S(1)}, bf16[4,2048,256]{2,1,0:T(8,128)(2,1)}, u32[]{:S(2)}) copy-start(bf16[4,2048,256]{2,1,0:T(8,128)(2,1)} %get-tuple-element.443) | copy-start | bytes 12582916 | tf_op jit(solution)/shard_map/while
  98.0 6.8 %collective-permute-start.4 = (bf16[1,2,64,256]{3,2,1,0:T(8,128)(2,1)S(1)}, bf16[1,2,64,256]{3,2,1,0:T(8,128)(2,1)S(1)}, u32[]{:S(2)}, u32[]{:S(2)}) collective-permute-start(bf16[1,2,64,256]{3,2,1,0:T(8,128)(2,1)S(1)} %bitcast.231), channel_id=1, source_target_pairs={{0,4},{4,8},{8,12},{12,16},{16,20},{20,24},{24,28},{28,0},{1,5},{5... | collective-permute-start | bytes 196616 | tf_op jit(solution)/shard_map/ppermute | solution.py:30
  98.3 6.5 %collective-permute-start.5 = (bf16[1,2,64,256]{3,2,1,0:T(8,128)(2,1)S(1)}, bf16[1,2,64,256]{3,2,1,0:T(8,128)(2,1)S(1)}, u32[]{:S(2)}, u32[]{:S(2)}) collective-permute-start(bf16[1,2,64,256]{3,2,1,0:T(8,128)(2,1)S(1)} %bitcast.230), channel_id=1, source_target_pairs={{4,0},{8,4},{12,8},{16,12},{20,16},{24,20},{28,24},{0,28},{5,1},{9... | collective-permute-start | bytes 196616 | tf_op jit(solution)/shard_map/ppermute | solution.py:31
  104.9 5.1 %collective-permute-start.6 = (bf16[4,1,64,256]{3,2,1,0:T(8,128)(2,1)S(1)}, bf16[4,1,64,256]{3,2,1,0:T(8,128)(2,1)S(1)}, u32[]{:S(2)}, u32[]{:S(2)}) collective-permute-start(bf16[4,1,64,256]{3,2,1,0:T(8,128)(2,1)S(1)} %get-tuple-element.262), channel_id=1, source_target_pairs={{0,1},{1,2},{2,3},{3,0},{4,5},{5,6},{6,7},{7,4},{8,9},{9,10},{10,1... | collective-permute-start | bytes 393224 | tf_op jit(solution)/shard_map/ppermute | solution.py:30
  105.5 4.7 %collective-permute-start.7 = (bf16[4,1,64,256]{3,2,1,0:T(8,128)(2,1)S(1)}, bf16[4,1,64,256]{3,2,1,0:T(8,128)(2,1)S(1)}, u32[]{:S(2)}, u32[]{:S(2)}) collective-permute-start(bf16[4,1,64,256]{3,2,1,0:T(8,128)(2,1)S(1)} %get-tuple-element.261), channel_id=1, source_target_pairs={{1,0},{2,1},{3,2},{0,3},{5,4},{6,5},{7,6},{4,7},{9,8},{10,9},{11,1... | collective-permute-start | bytes 393224 | tf_op jit(solution)/shard_map/ppermute | solution.py:31
  110.6 2.4 copy-start.10
  115.4 6.3 %copy-start.2 = (f32[2048,512]{1,0:T(8,128)}, f32[2048,512]{1,0:T(8,128)S(1)}, u32[]{:S(2)}) copy-start(f32[2048,512]{1,0:T(8,128)S(1)} %fusion.88) | copy-start | bytes 12582916 | tf_op jit(solution)/shard_map/while
  115.4 3.7 %copy-start.5 = (bf16[4,2048,256]{2,1,0:T(8,128)(2,1)S(1)}, bf16[4,2048,256]{2,1,0:T(8,128)(2,1)}, u32[]{:S(2)}) copy-start(bf16[4,2048,256]{2,1,0:T(8,128)(2,1)} %get-tuple-element.479) | copy-start | bytes 12582916 | tf_op jit(solution)/shard_map/while
  129.6 6.3 %copy-start.2 = (f32[2048,512]{1,0:T(8,128)}, f32[2048,512]{1,0:T(8,128)S(1)}, u32[]{:S(2)}) copy-start(f32[2048,512]{1,0:T(8,128)S(1)} %fusion.88) | copy-start | bytes 12582916 | tf_op jit(solution)/shard_map/while
  129.6 3.7 %copy-start.5 = (bf16[4,2048,256]{2,1,0:T(8,128)(2,1)S(1)}, bf16[4,2048,256]{2,1,0:T(8,128)(2,1)}, u32[]{:S(2)}) copy-start(bf16[4,2048,256]{2,1,0:T(8,128)(2,1)} %get-tuple-element.479) | copy-start | bytes 12582916 | tf_op jit(solution)/shard_map/while
  143.8 6.3 %copy-start.2 = (f32[2048,512]{1,0:T(8,128)}, f32[2048,512]{1,0:T(8,128)S(1)}, u32[]{:S(2)}) copy-start(f32[2048,512]{1,0:T(8,128)S(1)} %fusion.88) | copy-start | bytes 12582916 | tf_op jit(solution)/shard_map/while
  143.8 3.7 %copy-start.5 = (bf16[4,2048,256]{2,1,0:T(8,128)(2,1)S(1)}, bf16[4,2048,256]{2,1,0:T(8,128)(2,1)}, u32[]{:S(2)}) copy-start(bf16[4,2048,256]{2,1,0:T(8,128)(2,1)} %get-tuple-element.479) | copy-start | bytes 12582916 | tf_op jit(solution)/shard_map/while
  158.0 6.3 %copy-start.2 = (f32[2048,512]{1,0:T(8,128)}, f32[2048,512]{1,0:T(8,128)S(1)}, u32[]{:S(2)}) copy-start(f32[2048,512]{1,0:T(8,128)S(1)} %fusion.88) | copy-start | bytes 12582916 | tf_op jit(solution)/shard_map/while
  158.0 3.7 %copy-start.5 = (bf16[4,2048,256]{2,1,0:T(8,128)(2,1)S(1)}, bf16[4,2048,256]{2,1,0:T(8,128)(2,1)}, u32[]{:S(2)}) copy-start(bf16[4,2048,256]{2,1,0:T(8,128)(2,1)} %get-tuple-element.479) | copy-start | bytes 12582916 | tf_op jit(solution)/shard_map/while
  169.8 6.9 %copy-start.17 = (bf16[169,8192]{1,0:T(8,128)(2,1)S(1)}, bf16[169,8192]{1,0:T(8,128)(2,1)}, u32[]{:S(2)}) copy-start(bf16[169,8192]{1,0:T(8,128)(2,1)} %param.27) | copy-start | bytes 8306692
  169.8 6.9 %copy-start.18 = (bf16[256,169]{0,1:T(8,128)(2,1)S(1)}, bf16[256,169]{0,1:T(8,128)(2,1)}, u32[]{:S(2)}) copy-start(bf16[256,169]{0,1:T(8,128)(2,1)} %param.26) | copy-start | bytes 259588
  179.9 9.6 %copy-start.14 = (f32[1,256]{1,0:T(1,128)S(1)}, f32[1,256]{1,0:T(1,128)}, u32[]{:S(2)}) copy-start(f32[1,256]{1,0:T(1,128)} %get-tuple-element.269) | copy-start | bytes 3076
Sparse Core Ops, SparseCore 0:
  189.6 148.8 all-reduce.2
where the time goes:
time: 350 us; the launch traced here: 349 us
  waiting for transfers between devices  154 us (44%)
  matrix products  122 us (35%)
  local copies, waits for them, and re-layouts  34.6 us (10%)
  starting transfers between devices  18.3 us (5%)
  between operations  15.2 us (4%)
  other arithmetic  4.44 us (1%)
    psum x1, waiting for transfers between devices, body(): grad_in, grad_out = lax.psum((grad_in, grad_out), ('rep', 'gx', 'gy'))  148 us
    dot_general x8, matrix products, one_block(): lax.dot_general(target_hot.astype(jnp.float32), weighted, (((0,), (0,)),...  43.6 us
    dot_general x8, matrix products, one_block(): gathered = jnp.dot(source_hot, table, preferred_element_type=jnp.float32)  24.1 us
    dot_general x8, matrix products, one_block(): jnp.dot(edge_rows, weight_edge, preferred_element_type=jnp.float32)  20.7 us
    while x32, local copies, waits for them, and re-layouts  16.4 us
    dot_general x8, matrix products, one_block(): jnp.dot(target_hot, query_part, preferred_element_type=jnp.float32)  13 us
    ppermute x4, starting transfers between devices, with_halo(): after = lax.ppermute(initial, axis, down)  12.6 us
    dot_general x1, matrix products, body(): lax.dot_general(edges, dact, (((0,), (0,)), ((), ())), preferred_element_...  9.24 us
  transfers between devices with their start and end apart: 9, of which 5 were waited for; matrix products, arithmetic and copies ran while one was open for 2% of the time, Pallas kernels for 0%

commit v1 on v0

--- a/solution.py
+++ b/solution.py
@@ -148,7 +148,7 @@
     grad_out = lax.dot_general(
         hidden_head, dpred, (((0,), (1,)), ((), ())), preferred_element_type=jnp.float32
     )
-    grad_in, grad_out = lax.psum((grad_in, grad_out), ("rep", "gx", "gy"))
+    grad_in, grad_out = lax.psum(lax.psum((grad_in, grad_out), "rep"), ("gx", "gy"))
     return (nodes, grad_in, grad_out)
 
 

time: 350 us -> 588 us (1.68)
  the two profiles are of different devices: /device:TPU:1 before, /device:TPU:2 now
where the time goes in v1:
time: 588 us; the launch traced here: 587 us
  waiting for transfers between devices  393 us (67%)
  matrix products  122 us (21%)
  local copies, waits for them, and re-layouts  34.6 us (6%)
  starting transfers between devices  16.9 us (3%)
  between operations  15.2 us (3%)
    psum x1, waiting for transfers between devices, body(): lax.psum(lax.psum((grad_in, grad_out), 'rep'), ('gx', 'gy'))  345 us
    dot_general x8, matrix products, one_block(): lax.dot_general(target_hot.astype(jnp.float32), weighted, (((0,), (0,)),...  43.7 us
    psum x1, waiting for transfers between devices, body(): lax.psum((grad_in, grad_out), 'rep')  39.4 us
    dot_general x8, matrix products, one_block(): gathered = jnp.dot(source_hot, table, preferred_element_type=jnp.float32)  24.1 us
    dot_general x8, matrix products, one_block(): jnp.dot(edge_rows, weight_edge, preferred_element_type=jnp.float32)  20.7 us
    while x32, local copies, waits for them, and re-layouts  16.4 us
    dot_general x8, matrix products, one_block(): jnp.dot(target_hot, query_part, preferred_element_type=jnp.float32)  13 us
  transfers between devices with their start and end apart: 10, of which 7 were waited for; matrix products, arithmetic and copies ran while one was open for 1% of the time, Pallas kernels for 0%

profile of v1, /device:TPU:2, one launch (start us, length us, event | category | flops | bytes accessed | tf_op | source)
XLA Modules:
  0.0 586.8 jit_solution(14415260752648051621)
XLA Ops:
  8.2 1.9 gather_fusion
  10.1 3.3 collective-permute-start
  13.3 3.6 collective-permute-start.1
  16.9 1.2 slice_bitcast_fusion
  22.1 1.6 collective-permute-start.2
  24.8 2.3 collective-permute-done.2
  32.2 2.2 broadcast.102.clone
  34.5 61.8 %while.26 = (s32[]{:T(128)}, f32[256,256]{1,0:T(8,128)S(1)}, bf16[4,2048,256]{2,1,0:T(8,128)(2,1)}, s32[4,2048]{1,0:T(4,128)S(1)}, f32[4,2048,1]{1,2,0:T(1,128)S...) while((s32[]{:T(128)}, f32[256,256]{1,0:T(8,128)S(1)}, ...), condition=%wide.region_1.2_spmd.clone, body=%wide.region_0.1_spmd.clone.sunk | while | flops 4306108416 | bytes 55403708 | solution.py:83
  34.5 3.6 fusion.83
  38.1 1.6 convolution_add_fusion.6
  39.8 2.0 copy-done.16
  41.8 2.6 bitcast_dynamic-update-slice_fusion.4
  44.5 5.5 fusion.84
  50.0 3.6 fusion.83
  53.6 1.6 convolution_add_fusion.6
  55.3 2.0 copy-done.16
  57.3 2.6 bitcast_dynamic-update-slice_fusion.4
  59.9 5.5 fusion.84
  65.4 3.6 fusion.83
  69.0 1.6 convolution_add_fusion.6
  70.7 2.0 copy-done.16
  72.7 2.6 bitcast_dynamic-update-slice_fusion.4
  75.3 5.5 fusion.84
  80.8 3.6 fusion.83
  84.5 1.6 convolution_add_fusion.6
  86.1 2.0 copy-done.16
  88.2 2.6 bitcast_dynamic-update-slice_fusion.4
  90.8 5.5 fusion.84
  97.9 1.3 collective-permute-start.4
  99.2 4.5 collective-permute-start.5
  103.7 2.2 collective-permute-done.4
  106.0 1.3 collective-permute-start.6
  108.4 2.6 collective-permute-done.6
  111.0 1.6 collective-permute-done.7
  113.1 2.3 broadcast.102
  115.4 56.8 %while.27 = (s32[]{:T(128)}, f32[256,256]{1,0:T(8,128)S(1)}, bf16[4,2048,256]{2,1,0:T(8,128)(2,1)}, s32[4,2048]{1,0:T(4,128)S(1)}, f32[4,2048,1]{1,2,0:T(1,128)S...) while((s32[]{:T(128)}, f32[256,256]{1,0:T(8,128)S(1)}, ...), condition=%wide.region_5.6_spmd.clone, body=%wide.region_4.5_spmd.clone.sunk | while | flops 4306108416 | bytes 55403708 | solution.py:83
  115.4 2.4 fusion.88
  117.9 1.6 convolution_add_fusion.7
  119.5 2.0 copy-done.5
  121.6 2.6 bitcast_dynamic-update-slice_fusion.5
  124.2 5.5 fusion.89
  129.7 2.4 fusion.88
  132.1 1.6 convolution_add_fusion.7
  133.7 2.0 copy-done.5
  135.8 2.5 bitcast_dynamic-update-slice_fusion.5
  138.3 5.5 fusion.89
  143.8 2.4 fusion.88
  146.2 1.6 convolution_add_fusion.7
  147.9 2.0 copy-done.5
  149.9 2.6 bitcast_dynamic-update-slice_fusion.5
  152.5 5.5 fusion.89
  158.0 2.4 fusion.88
  160.5 1.6 convolution_add_fusion.7
  162.1 2.0 copy-done.5
  164.1 2.6 bitcast_dynamic-update-slice_fusion.5
  166.7 5.5 fusion.89
  172.2 6.9 %multiply_convert_fusion = (bf16[8192,256]{1,0:T(8,128)(2,1)S(1)}, f32[8192,256]{1,0:T(8,128)}) fusion(bf16[8192,256]{1,0:T(8,128)(2,1)} %bitcast.214, bf16[256,256]{1,0:T(8,128)(2,1)S(1)} %copy-done), kind=kOutput, calls=%fused_computation.62 | convolution fusion | flops 1084227584 | bytes 16908288 | tf_op jit(solution)/shard_map/dot_general | solution.py:133
  179.1 1.6 fusion.39
  180.7 1.6 fusion.50
  182.3 9.2 %fusion.40 = f32[256,256]{1,0:T(8,128)} fusion(bf16[8192,256]{1,0:T(8,128)(2,1)} %bitcast.215, bf16[169,8192]{1,0:T(8,128)(2,1)S(1)} %fusion.39, bf16[256,169]{0,1:T(8,128)(2,1)S(1)} %copy-done.18, f32[8192,256]{1,0:T(8,128)} %get-tuple-element.274), kind=kOutput, calls=%fused_computation.64 | convolution fusion | flops 1801453568 | bytes 15700480 | tf_op jit(solution)/shard_map/dot_general | solution.py:145
  191.9 39.4 %all-reduce.7.cloned.1.call-done = (f32[256,256]{1,0:T(8,128)}, f32[256,169]{0,1:T(8,128)}) async-done(((f32[256,256]{1,0:T(8,128)}, f32[256,169]{0,1:T(8,128)}), (f32[256,256]{1,0:T(8,128)}, f32[256,169]{0,1:T(8,128)})) %all-reduce.7.cloned.1.call-update) | async-done | bytes 435216 | tf_op jit(solution)/shard_map/psum | solution.py:151
  232.1 344.6 %all-reduce.5.cloned.1.call-done = (f32[256,256]{1,0:T(8,128)}, f32[256,169]{0,1:T(8,128)}) async-done(((f32[256,256]{1,0:T(8,128)}, f32[256,169]{0,1:T(8,128)}), (f32[256,256]{1,0:T(8,128)}, f32[256,169]{0,1:T(8,128)})) %all-reduce.5.cloned.1.call-update) | async-done | bytes 435216 | tf_op jit(solution)/shard_map/psum | solution.py:151
  576.7 1.7 copy.62
  578.4 1.6 copy.63
  (143 shorter events, 15.2 us)
Async XLA Ops:
  7.2 165.0 %copy-start = (bf16[256,256]{1,0:T(8,128)(2,1)S(1)}, bf16[256,256]{1,0:T(8,128)(2,1)}, u32[]{:S(2)}) copy-start(bf16[256,256]{1,0:T(8,128)(2,1)} %param.25) | copy-start | bytes 393220
  7.2 10.9 %copy-start.3 = (bf16[256,256]{1,0:T(8,128)(2,1)S(1)}, bf16[256,256]{1,0:T(8,128)(2,1)}, u32[]{:S(2)}) copy-start(bf16[256,256]{1,0:T(8,128)(2,1)} %param.16) | copy-start | bytes 393220
  7.2 10.9 %copy-start.6 = (bf16[2,256,768]{2,1,0:T(8,128)(2,1)S(1)}, bf16[2,256,768]{2,1,0:T(8,128)(2,1)}, u32[]{:S(2)}) copy-start(bf16[2,256,768]{2,1,0:T(8,128)(2,1)} %param.22) | copy-start | bytes 2359300
  7.2 11.8 %copy-start.7 = (bf16[2,256,256]{2,1,0:T(8,128)(2,1)S(1)}, bf16[2,256,256]{2,1,0:T(8,128)(2,1)}, u32[]{:S(2)}) copy-start(bf16[2,256,256]{2,1,0:T(8,128)(2,1)} %param.23) | copy-start | bytes 786436
  7.2 12.6 %copy-start.12 = (s32[8192]{0:T(1024)S(1)}, s32[8192]{0:T(1024)}, u32[]{:S(2)}) copy-start(s32[8192]{0:T(1024)} %param.19) | copy-start | bytes 98308
  7.2 12.6 %copy-start.13 = (s32[8192]{0:T(1024)S(1)}, s32[8192]{0:T(1024)}, u32[]{:S(2)}) copy-start(s32[8192]{0:T(1024)} %param.18) | copy-start | bytes 98308
  7.2 224.1 %all-reduce.7.cloned.1.call-start = ((), (), s32[]{:S(2)}) async-start(), calls=%async_computation.1 | async-start | bytes 884736 | tf_op jit(solution)/shard_map/psum | solution.py:151
  10.0 13.6 %copy-start.15 = (f32[2,256]{1,0:T(2,128)S(1)}, f32[2,256]{1,0:T(2,128)}, u32[]{:S(2)}) copy-start(f32[2,256]{1,0:T(2,128)} %param.24) | copy-start | bytes 6148
  10.1 9.8 %collective-permute-start = (bf16[1,2,64,256]{3,2,1,0:T(8,128)(2,1)S(1)}, bf16[1,2,64,256]{3,2,1,0:T(8,128)(2,1)S(1)}, u32[]{:S(2)}, u32[]{:S(2)}) collective-permute-start(bf16[1,2,64,256]{3,2,1,0:T(8,128)(2,1)S(1)} %bitcast.229), channel_id=1, source_target_pairs={{0,4},{4,8},{8,12},{12,16},{16,20},{20,24},{24,28},{28,0},{1,5},{5... | collective-permute-start | bytes 196616 | tf_op jit(solution)/shard_map/ppermute | solution.py:30
  13.3 6.6 %collective-permute-start.1 = (bf16[1,2,64,256]{3,2,1,0:T(8,128)(2,1)S(1)}, bf16[1,2,64,256]{3,2,1,0:T(8,128)(2,1)S(1)}, u32[]{:S(2)}, u32[]{:S(2)}) collective-permute-start(bf16[1,2,64,256]{3,2,1,0:T(8,128)(2,1)S(1)} %bitcast.228), channel_id=1, source_target_pairs={{4,0},{8,4},{12,8},{16,12},{20,16},{24,20},{28,24},{0,28},{5,1},{9... | collective-permute-start | bytes 196616 | tf_op jit(solution)/shard_map/ppermute | solution.py:31
  18.4 13.9 %copy-start.4 = (bf16[256,768]{1,0:T(8,128)(2,1)}, bf16[256,768]{1,0:T(8,128)(2,1)S(1)}, u32[]{:S(2)}) copy-start(bf16[256,768]{1,0:T(8,128)(2,1)S(1)} %convolution_convert_fusion.3) | copy-start | bytes 1179652
  19.9 0.6 copy-start.9
  20.5 0.6 copy-start.8
  22.1 5.0 collective-permute-start.2
  24.2 5.0 collective-permute-start.3
  31.2 3.3 copy-start.11
  32.2 2.2 slice-start
  38.1 6.3 %copy-start.1 = (f32[2048,512]{1,0:T(8,128)}, f32[2048,512]{1,0:T(8,128)S(1)}, u32[]{:S(2)}) copy-start(f32[2048,512]{1,0:T(8,128)S(1)} %fusion.83) | copy-start | bytes 12582916 | tf_op jit(solution)/shard_map/while
  38.1 3.7 copy-start.16
  53.6 6.3 %copy-start.1 = (f32[2048,512]{1,0:T(8,128)}, f32[2048,512]{1,0:T(8,128)S(1)}, u32[]{:S(2)}) copy-start(f32[2048,512]{1,0:T(8,128)S(1)} %fusion.83) | copy-start | bytes 12582916 | tf_op jit(solution)/shard_map/while
  53.6 3.7 copy-start.16
  69.0 6.3 %copy-start.1 = (f32[2048,512]{1,0:T(8,128)}, f32[2048,512]{1,0:T(8,128)S(1)}, u32[]{:S(2)}) copy-start(f32[2048,512]{1,0:T(8,128)S(1)} %fusion.83) | copy-start | bytes 12582916 | tf_op jit(solution)/shard_map/while
  69.0 3.7 copy-start.16
  84.5 6.3 %copy-start.1 = (f32[2048,512]{1,0:T(8,128)}, f32[2048,512]{1,0:T(8,128)S(1)}, u32[]{:S(2)}) copy-start(f32[2048,512]{1,0:T(8,128)S(1)} %fusion.83) | copy-start | bytes 12582916 | tf_op jit(solution)/shard_map/while
  84.5 3.7 copy-start.16
  97.9 7.9 %collective-permute-start.4 = (bf16[1,2,64,256]{3,2,1,0:T(8,128)(2,1)S(1)}, bf16[1,2,64,256]{3,2,1,0:T(8,128)(2,1)S(1)}, u32[]{:S(2)}, u32[]{:S(2)}) collective-permute-start(bf16[1,2,64,256]{3,2,1,0:T(8,128)(2,1)S(1)} %bitcast.231), channel_id=1, source_target_pairs={{0,4},{4,8},{8,12},{12,16},{16,20},{20,24},{24,28},{28,0},{1,5},{5... | collective-permute-start | bytes 196616 | tf_op jit(solution)/shard_map/ppermute | solution.py:30
  99.2 6.7 %collective-permute-start.5 = (bf16[1,2,64,256]{3,2,1,0:T(8,128)(2,1)S(1)}, bf16[1,2,64,256]{3,2,1,0:T(8,128)(2,1)S(1)}, u32[]{:S(2)}, u32[]{:S(2)}) collective-permute-start(bf16[1,2,64,256]{3,2,1,0:T(8,128)(2,1)S(1)} %bitcast.230), channel_id=1, source_target_pairs={{4,0},{8,4},{12,8},{16,12},{20,16},{24,20},{28,24},{0,28},{5,1},{9... | collective-permute-start | bytes 196616 | tf_op jit(solution)/shard_map/ppermute | solution.py:31
  106.0 5.0 collective-permute-start.6
  107.6 5.0 collective-permute-start.7
  113.0 2.4 copy-start.10
  117.9 6.3 %copy-start.2 = (f32[2048,512]{1,0:T(8,128)}, f32[2048,512]{1,0:T(8,128)S(1)}, u32[]{:S(2)}) copy-start(f32[2048,512]{1,0:T(8,128)S(1)} %fusion.88) | copy-start | bytes 12582916 | tf_op jit(solution)/shard_map/while
  117.9 3.7 copy-start.5
  132.1 6.2 %copy-start.2 = (f32[2048,512]{1,0:T(8,128)}, f32[2048,512]{1,0:T(8,128)S(1)}, u32[]{:S(2)}) copy-start(f32[2048,512]{1,0:T(8,128)S(1)} %fusion.88) | copy-start | bytes 12582916 | tf_op jit(solution)/shard_map/while
  132.1 3.7 copy-start.5
  146.2 6.3 %copy-start.2 = (f32[2048,512]{1,0:T(8,128)}, f32[2048,512]{1,0:T(8,128)S(1)}, u32[]{:S(2)}) copy-start(f32[2048,512]{1,0:T(8,128)S(1)} %fusion.88) | copy-start | bytes 12582916 | tf_op jit(solution)/shard_map/while
  146.2 3.7 copy-start.5
  160.4 6.3 %copy-start.2 = (f32[2048,512]{1,0:T(8,128)}, f32[2048,512]{1,0:T(8,128)S(1)}, u32[]{:S(2)}) copy-start(f32[2048,512]{1,0:T(8,128)S(1)} %fusion.88) | copy-start | bytes 12582916 | tf_op jit(solution)/shard_map/while
  160.4 3.7 copy-start.5
  172.2 6.9 %copy-start.17 = (bf16[169,8192]{1,0:T(8,128)(2,1)S(1)}, bf16[169,8192]{1,0:T(8,128)(2,1)}, u32[]{:S(2)}) copy-start(bf16[169,8192]{1,0:T(8,128)(2,1)} %param.27) | copy-start | bytes 8306692
  172.2 6.9 %copy-start.18 = (bf16[256,169]{0,1:T(8,128)(2,1)S(1)}, bf16[256,169]{0,1:T(8,128)(2,1)}, u32[]{:S(2)}) copy-start(bf16[256,169]{0,1:T(8,128)(2,1)} %param.26) | copy-start | bytes 259588
  182.3 49.0 %copy-start.14 = (f32[1,256]{1,0:T(1,128)S(1)}, f32[1,256]{1,0:T(1,128)}, u32[]{:S(2)}) copy-start(f32[1,256]{1,0:T(1,128)} %get-tuple-element.271) | copy-start | bytes 3076
  191.6 385.2 %all-reduce.5.cloned.1.call-start = ((), (), s32[]{:S(2)}) async-start(), calls=%async_computation | async-start | bytes 884736 | tf_op jit(solution)/shard_map/psum | solution.py:151
Sparse Core Ops, SparseCore 0:
  191.7 39.5 all-reduce.6
  234.0 342.6 all-reduce.4
